TPU v7x, 512 devices: a whole 4x4x16 slice. The times are simulated.
512 devices in a mesh: dp: 8 (over z_lo), pipe: 4 (over x), seq: 16 (over z_hi, y, core).
Axes of the slice: x: 4, y: 4, z: 16 (z_hi: 2, z_lo: 8; z = z_hi * 8 + z_lo), core: 2. Of those that a mesh axis runs over, the one named last changes fastest.
Arguments:
- queries: bfloat16 [4, 8, 2048, 2048], P('pipe', 'dp', 'seq'), may hold values from -6 to 6
- keys: bfloat16 [4, 8, 2048, 512], P('pipe', 'dp', 'seq'), may hold values from -6 to 6
- values: bfloat16 [4, 8, 2048, 512], P('pipe', 'dp', 'seq'), may hold values from -6 to 6
- grad_next: bfloat16 [4, 8, 2048, 2048], P('pipe', 'dp', 'seq'), may hold values from -6 to 6
- normed: bfloat16 [4, 8, 2048, 4096], P('pipe', 'dp', 'seq'), may hold values from -6 to 6
- value_weight: bfloat16 [4, 4096, 512], P('pipe', 'seq'), may hold values from -0.09375 to 0.09375
Outputs:
- grad_queries: bfloat16 [4, 8, 2048, 2048], P('pipe', 'dp', 'seq')
- grad_keys: bfloat16 [4, 8, 2048, 512], P('pipe', 'dp', 'seq')
- grad_normed: bfloat16 [4, 8, 2048, 4096], P('pipe', 'dp', 'seq')
- grad_value_weight: float32 [4, 4096, 512], P('pipe', 'seq')
All inputs are finite; a program needn't handle non-finite values.
Results may differ from a plain program's by a relative error of at most 0.019.
Values may be sent and summed in bfloat16 or wider, within the bound.
A program may use at most 64 MiB of HBM per device.

v0:
```python
import jax
import jax.numpy as jnp
from jax import lax
from jax.sharding import PartitionSpec as P

HEAD = 128
HQ = 16


masked_value = -1e30


def passed_along(block, axis, distance):
    devices = range(lax.axis_size(axis))
    route = [((i - distance) % len(devices), i) for i in devices]
    return lax.ppermute(block, axis, route)


def attend(query_head, key_head, value_head, upstream_head):
    length = query_head.shape[0]
    block_rows = min(512, length)
    factor = HEAD ** (-0.5)
    query_parts = []
    grad_key = jnp.zeros((length, HEAD), jnp.float32)
    grad_value = jnp.zeros((length, HEAD), jnp.float32)
    for block_index in range(length // block_rows):
        first_row = block_index * block_rows
        finish = first_row + block_rows
        query_block = query_head[first_row:finish]
        upstream_block = upstream_head[first_row:finish]
        key_prefix = key_head[:finish]
        value_prefix = value_head[:finish]
        row_pos = first_row + jnp.arange(block_rows, dtype=jnp.int32)[:, None]
        col_pos = jnp.arange(finish, dtype=jnp.int32)[None, :]
        scores = jnp.where(
            col_pos <= row_pos,
            lax.dot_general(
                query_block,
                key_prefix,
                (((1,), (1,)), ((), ())),
                preferred_element_type=jnp.float32,
            )
            * factor,
            masked_value,
        )
        row_top = jnp.max(scores, axis=1, keepdims=True)
        row_total = jnp.sum(jnp.exp(scores - row_top), axis=1, keepdims=True)
        probs_half = (jnp.exp(scores - row_top) / row_total).astype(jnp.bfloat16)
        attn_out = jnp.dot(probs_half, value_prefix, preferred_element_type=jnp.float32)
        row_delta = jnp.sum(upstream_block.astype(jnp.float32) * attn_out, axis=1, keepdims=True)
        grad_probs = lax.dot_general(
            upstream_block,
            value_prefix,
            (((1,), (1,)), ((), ())),
            preferred_element_type=jnp.float32,
        )
        grad_scores = (jnp.exp(scores - row_top) / row_total * (grad_probs - row_delta)).astype(
            jnp.bfloat16
        )
        query_parts.append(
            jnp.dot(grad_scores, key_prefix, preferred_element_type=jnp.float32) * factor
        )
        key_part = (
            lax.dot_general(
                grad_scores,
                query_block,
                (((0,), (0,)), ((), ())),
                preferred_element_type=jnp.float32,
            )
            * factor
        )
        value_part = lax.dot_general(
            probs_half, upstream_block, (((0,), (0,)), ((), ())), preferred_element_type=jnp.float32
        )
        grad_key = grad_key.at[:finish].add(key_part)
        grad_value = grad_value.at[:finish].add(value_part)
    return (jnp.concatenate(query_parts, axis=0), grad_key, grad_value)


def local(queries, keys, values, grad_next, normed, value_weight):
    query_rows = queries[0, 0]
    key_rows = keys[0, 0]
    value_rows = values[0, 0]
    normed_rows = normed[0, 0]
    value_proj = value_weight[0]
    upstream = passed_along(grad_next[0, 0], "pipe", -1)
    tokens = query_rows.shape[0]
    kv_heads = key_rows.shape[1] // HEAD
    repeats = HQ // kv_heads

    def widen(source):
        spread = jnp.broadcast_to(
            source.reshape(tokens, kv_heads, 1, HEAD), (tokens, kv_heads, repeats, HEAD)
        )
        return spread.reshape(tokens, kv_heads * repeats * HEAD)

    query_cols, key_cols, value_cols, upstream_cols = (
        lax.all_to_all(query_rows, "seq", split_axis=1, concat_axis=0, tiled=True),
        lax.all_to_all(widen(key_rows), "seq", split_axis=1, concat_axis=0, tiled=True),
        lax.all_to_all(widen(value_rows), "seq", split_axis=1, concat_axis=0, tiled=True),
        lax.all_to_all(upstream, "seq", split_axis=1, concat_axis=0, tiled=True),
    )
    head_grads = [attend(query_cols, key_cols, value_cols, upstream_cols)]
    query_terms = jnp.concatenate([entry[0] for entry in head_grads], axis=1).astype(jnp.bfloat16)
    key_terms = jnp.concatenate([entry[1] for entry in head_grads], axis=1).astype(jnp.bfloat16)
    value_terms = jnp.concatenate([entry[2] for entry in head_grads], axis=1).astype(jnp.bfloat16)
    back_query, back_key, back_value = (
        lax.all_to_all(query_terms, "seq", split_axis=0, concat_axis=1, tiled=True),
        lax.all_to_all(key_terms, "seq", split_axis=0, concat_axis=1, tiled=True),
        lax.all_to_all(value_terms, "seq", split_axis=0, concat_axis=1, tiled=True),
    )

    def grouped(head_terms):
        summed = head_terms.astype(jnp.float32).reshape(tokens, kv_heads, repeats, HEAD).sum(axis=2)
        return summed.reshape(tokens, kv_heads * HEAD).astype(jnp.bfloat16)

    key_grad_rows = grouped(back_key)
    value_grad_rows = grouped(back_value)
    normed_cols = lax.all_to_all(normed_rows, "seq", split_axis=1, concat_axis=0, tiled=True)
    all_value_grads = lax.all_gather(value_grad_rows, "seq", axis=0, tiled=True)
    weight_term = lax.dot_general(
        normed_cols, all_value_grads, (((0,), (0,)), ((), ())), preferred_element_type=jnp.float32
    )
    weight_grad = lax.psum(weight_term.astype(jnp.bfloat16), "dp").astype(jnp.float32)
    full_rows = lax.dot_general(
        value_grad_rows,
        lax.all_gather(value_proj, "seq", axis=0, tiled=True),
        (((1,), (1,)), ((), ())),
        preferred_element_type=jnp.float32,
    )
    input_grad = full_rows.astype(jnp.bfloat16)
    return (
        back_query[None, None],
        key_grad_rows[None, None],
        input_grad[None, None],
        weight_grad[None],
    )


def solution(mesh):
    placed = (
        P("pipe", "dp", "seq", None),
        P("pipe", "dp", "seq", None),
        P("pipe", "dp", "seq", None),
        P("pipe", "dp", "seq", None),
        P("pipe", "dp", "seq", None),
        P("pipe", "seq", None),
    )
    return jax.shard_map(
        local,
        mesh=mesh,
        in_specs=placed,
        out_specs=(
            P("pipe", "dp", "seq", None),
            P("pipe", "dp", "seq", None),
            P("pipe", "dp", "seq", None),
            P("pipe", "seq", None),
        ),
        check_vma=False,
    )
```

profile of v0, /device:TPU:6, one launch (start us, length us, event | category | flops | bytes accessed | tf_op | source)
XLA Modules:
  0.0 549.3 jit_solution(11475916848880484211)
XLA Ops:
  7.2 1.0 broadcast_in_dim.33
  8.2 0.9 broadcast_in_dim.34
  9.1 17.8 %all-to-all-start.1 = ((bf16[128,16,128]{2,0,1:T(8,128)(2,1)}), bf16[128,16,128]{2,0,1:T(8,128)(2,1)S(1)}, u32[]{:S(2)}, u32[]{:S(2)}) async-start(bf16[128,16,128]{2,0,1:T(8,128)(2,1)} %bitcast.3), calls=%async_computation.1 | async-start | bytes 1048576 | tf_op jit(solution)/shard_map/all_to_all | solution.py:99
  27.0 1.0 copy.50
  28.0 19.1 %all-to-all-done.1 = bf16[128,16,128]{2,0,1:T(8,128)(2,1)S(1)} async-done(((bf16[128,16,128]{2,0,1:T(8,128)(2,1)}), bf16[128,16,128]{2,0,1:T(8,128)(2,1)S(1)}, u32[]{:S(2)}, u32[]{:S(2)}) %all-to-all-start.1) | async-done | bytes 524320 | tf_op jit(solution)/shard_map/all_to_all | solution.py:99
  47.0 3.6 all-to-all-start
  50.6 2.7 collective-permute-start
  53.4 14.4 %collective-permute-done = bf16[128,2048]{1,0:T(8,128)(2,1)S(1)} collective-permute-done((bf16[128,2048]{1,0:T(8,128)(2,1)S(1)}, bf16[128,2048]{1,0:T(8,128)(2,1)S(1)}, u32[]{:S(2)}, u32[]{:S(2)}) %collective-permute-start) | collective-permute-done | bytes 524320 | tf_op jit(solution)/shard_map/ppermute | solution.py:16
  67.8 1.0 copy.53
  68.9 1.2 all-to-all-done
  70.1 13.1 %all-to-all-start.2 = ((bf16[128,16,128]{0,2,1:T(8,128)(2,1)}), bf16[128,16,128]{0,2,1:T(8,128)(2,1)}, u32[]{:S(2)}, u32[]{:S(2)}) async-start(bf16[128,16,128]{0,2,1:T(8,128)(2,1)} %bitcast.7), calls=%async_computation.2 | async-start | bytes 1048576 | tf_op jit(solution)/shard_map/all_to_all | solution.py:101
  85.4 0.8 fusion.62
  86.8 1.0 fusion.61
  88.0 1.0 fusion.40
  90.3 2.7 fusion.2
  93.0 9.8 %all-to-all-done.2 = bf16[128,16,128]{0,2,1:T(8,128)(2,1)} async-done(((bf16[128,16,128]{0,2,1:T(8,128)(2,1)}), bf16[128,16,128]{0,2,1:T(8,128)(2,1)}, u32[]{:S(2)}, u32[]{:S(2)}) %all-to-all-start.2) | async-done | bytes 524320 | tf_op jit(solution)/shard_map/all_to_all | solution.py:101
  102.9 1.3 slice_bitcast_fusion.3
  104.2 1.4 fusion.47
  105.7 0.8 fusion.20
  106.5 0.7 fusion.9
  107.2 1.5 copy-done
  108.7 0.8 fusion.14
  109.5 23.9 %all_to_all.128 = bf16[16,128,128]{2,1,0:T(8,128)(2,1)S(1)} all-to-all(bf16[16,128,128]{2,1,0:T(8,128)(2,1)S(1)} %bitcast.130), channel_id=1, replica_groups=mesh['dp'=8,'pipe'=4,'seq'=16] {'seq'}, dimensions={0} | all-to-all | bytes 1048576 | tf_op jit(solution)/shard_map/all_to_all | solution.py:110
  133.4 0.7 bitcast_reduce_fusion
  134.1 1.6 copy.65
  135.8 1.6 broadcast_in_dim.36
  137.4 0.9 copy.55
  138.3 0.9 broadcast_in_dim.37
  139.2 6.6 %all-to-all-start.3 = ((bf16[128,16,128]{2,0,1:T(8,128)(2,1)}), bf16[128,16,128]{2,0,1:T(8,128)(2,1)}, u32[]{:S(2)}, u32[]{:S(2)}) async-start(bf16[128,16,128]{2,0,1:T(8,128)(2,1)} %bitcast.131), calls=%async_computation.3 | async-start | bytes 1048576 | tf_op jit(solution)/shard_map/all_to_all | solution.py:100
  145.8 2.3 copy.66
  148.1 17.4 %all-to-all-done.3 = bf16[128,16,128]{2,0,1:T(8,128)(2,1)} async-done(((bf16[128,16,128]{2,0,1:T(8,128)(2,1)}), bf16[128,16,128]{2,0,1:T(8,128)(2,1)}, u32[]{:S(2)}, u32[]{:S(2)}) %all-to-all-start.3) | async-done | bytes 524320 | tf_op jit(solution)/shard_map/all_to_all | solution.py:100
  165.5 9.3 %all-to-all-start.7 = ((bf16[128,16,256]{0,2,1:T(8,128)(2,1)}), bf16[128,16,256]{0,2,1:T(8,128)(2,1)}, u32[]{:S(2)}, u32[]{:S(2)}) async-start(bf16[128,16,256]{0,2,1:T(8,128)(2,1)} %bitcast.122), calls=%async_computation.7 | async-start | bytes 2097152 | tf_op jit(solution)/shard_map/all_to_all | solution.py:119
  175.5 1.0 slice.254
  176.6 1.0 slice.259
  177.5 1.0 slice.263
  178.6 1.4 fusion.30
  180.3 0.8 copy-done.12
  182.2 0.9 copy-done.16
  183.8 0.8 multiply_convert_fusion.1
  185.6 0.8 copy-done.1
  186.4 1.9 fusion.31
  188.9 1.1 copy-done.2
  190.1 0.7 fusion.11
  190.8 2.0 multiply_convert_fusion
  192.8 1.3 copy-done.4
  194.2 1.6 fusion.13
  195.8 13.4 %all-to-all-done.7 = bf16[128,16,256]{0,2,1:T(8,128)(2,1)} async-done(((bf16[128,16,256]{0,2,1:T(8,128)(2,1)}), bf16[128,16,256]{0,2,1:T(8,128)(2,1)}, u32[]{:S(2)}, u32[]{:S(2)}) %all-to-all-start.7) | async-done | bytes 1048608 | tf_op jit(solution)/shard_map/all_to_all | solution.py:119
  209.2 13.0 %all-to-all-start.5 = ((bf16[16,128,128]{2,1,0:T(8,128)(2,1)}), bf16[16,128,128]{2,1,0:T(8,128)(2,1)}, u32[]{:S(2)}, u32[]{:S(2)}) async-start(bf16[16,128,128]{2,1,0:T(8,128)(2,1)} %bitcast.134), calls=%async_computation.5 | async-start | bytes 1048576 | tf_op jit(solution)/shard_map/all_to_all | solution.py:109
  222.2 1.4 fusion.24
  223.6 1.4 fusion.27
  225.7 0.7 fusion.25
  226.4 0.8 pad_maximum_fusion
  227.2 49.0 %all-to-all-done.5 = bf16[16,128,128]{2,1,0:T(8,128)(2,1)} async-done(((bf16[16,128,128]{2,1,0:T(8,128)(2,1)}), bf16[16,128,128]{2,1,0:T(8,128)(2,1)}, u32[]{:S(2)}, u32[]{:S(2)}) %all-to-all-start.5) | async-done | bytes 524320 | tf_op jit(solution)/shard_map/all_to_all | solution.py:109
  276.2 4.4 all-to-all-start.4
  280.6 1.5 copy.67
  282.1 1.1 bitcast_reduce_fusion.1
  283.3 0.8 copy.68
  284.1 18.8 %all-to-all-done.4 = bf16[16,128,128]{2,1,0:T(8,128)(2,1)S(1)} async-done(((bf16[16,128,128]{2,1,0:T(8,128)(2,1)}), bf16[16,128,128]{2,1,0:T(8,128)(2,1)S(1)}, u32[]{:S(2)}, u32[]{:S(2)}) %all-to-all-start.4) | async-done | bytes 524320 | tf_op jit(solution)/shard_map/all_to_all | solution.py:108
  303.2 1.0 broadcast_in_dim.71
  304.2 3.0 fusion.23
  307.3 113.7 %all-gather.6.cloned.1.call-done = bf16[1,4096,512]{2,1,0:T(8,128)(2,1)} async-done(((bf16[1,256,512]{2,1,0:T(8,128)(2,1)}), bf16[1,4096,512]{2,1,0:T(8,128)(2,1)}) %all-gather.6.cloned.1.call-update) | async-done | bytes 4194320 | tf_op jit(solution)/shard_map/all_gather | solution.py:127
  421.0 4.6 fusion
  425.6 115.2 %all-reduce.4.cloned.1.call-done = bf16[1,256,512]{1,2,0:T(8,128)(2,1)} async-done(((bf16[1,256,512]{1,2,0:T(8,128)(2,1)}), bf16[1,256,512]{1,2,0:T(8,128)(2,1)}) %all-reduce.4.cloned.1.call-update) | async-done | bytes 262160 | tf_op jit(solution)/shard_map/psum | solution.py:124
  540.9 1.9 copy.69
  (99 shorter events, 10.1 us)
Async XLA Ops:
  7.2 19.8 %copy-start.25 = (bf16[1,1,128,2048]{3,2,1,0:T(8,128)(2,1)S(1)}, bf16[1,1,128,2048]{3,2,1,0:T(8,128)(2,1)}, u32[]{:S(2)}) copy-start(bf16[1,1,128,2048]{3,2,1,0:T(8,128)(2,1)} %param.26) | copy-start | bytes 1572868
  8.2 42.4 %copy-start.33 = (bf16[1,1,128,2048]{3,2,1,0:T(8,128)(2,1)S(1)}, bf16[1,1,128,2048]{3,2,1,0:T(8,128)(2,1)}, u32[]{:S(2)}) copy-start(bf16[1,1,128,2048]{3,2,1,0:T(8,128)(2,1)} %param.29) | copy-start | bytes 1572868
  9.1 37.9 %all-to-all-start.1 = ((bf16[128,16,128]{2,0,1:T(8,128)(2,1)}), bf16[128,16,128]{2,0,1:T(8,128)(2,1)S(1)}, u32[]{:S(2)}, u32[]{:S(2)}) async-start(bf16[128,16,128]{2,0,1:T(8,128)(2,1)} %bitcast.3), calls=%async_computation.1 | async-start | bytes 1048576 | tf_op jit(solution)/shard_map/all_to_all | solution.py:99
  47.0 39.8 %copy-start.10 = (bf16[128,16,128]{2,0,1:T(8,128)(2,1)}, bf16[128,16,128]{2,0,1:T(8,128)(2,1)S(1)}, u32[]{:S(2)}) copy-start(bf16[128,16,128]{2,0,1:T(8,128)(2,1)S(1)} %all-to-all-done.1) | copy-start | bytes 1572868
  47.0 23.1 %all-to-all-start = ((bf16[128,16,128]{0,2,1:T(8,128)(2,1)}), bf16[128,16,128]{0,2,1:T(8,128)(2,1)S(1)}, u32[]{:S(2)}, u32[]{:S(2)}) async-start(bf16[128,16,128]{0,2,1:T(8,128)(2,1)} %bitcast), calls=%async_computation | async-start | bytes 1048576 | tf_op jit(solution)/shard_map/all_to_all | solution.py:98
  50.6 17.2 %collective-permute-start = (bf16[128,2048]{1,0:T(8,128)(2,1)S(1)}, bf16[128,2048]{1,0:T(8,128)(2,1)S(1)}, u32[]{:S(2)}, u32[]{:S(2)}) collective-permute-start(bf16[128,2048]{1,0:T(8,128)(2,1)S(1)} %bitcast.157), channel_id=1, source_target_pairs={{16,0},{32,16},{48,32},{0,48},{17,1},{33,17},{49,33},{1,49},{18,2}... | collective-permute-start | bytes 1572872 | tf_op jit(solution)/shard_map/ppermute | solution.py:16
  68.8 15.1 %copy-start.26 = (bf16[4,128,128]{2,1,0:T(8,128)(2,1)}, bf16[4,128,128]{2,1,0:T(8,128)(2,1)S(1)}, u32[]{:S(2)}) copy-start(bf16[4,128,128]{2,1,0:T(8,128)(2,1)S(1)} %slice.253) | copy-start | bytes 393220
  68.9 15.4 %copy-start.20 = (bf16[8,128,128]{2,1,0:T(8,128)(2,1)}, bf16[8,128,128]{2,1,0:T(8,128)(2,1)S(1)}, u32[]{:S(2)}) copy-start(bf16[8,128,128]{2,1,0:T(8,128)(2,1)S(1)} %slice.257) | copy-start | bytes 786436
  68.9 16.5 %copy-start.17 = (bf16[12,128,128]{2,1,0:T(8,128)(2,1)}, bf16[12,128,128]{2,1,0:T(8,128)(2,1)S(1)}, u32[]{:S(2)}) copy-start(bf16[12,128,128]{2,1,0:T(8,128)(2,1)S(1)} %slice.261) | copy-start | bytes 1179652
  70.1 32.7 %all-to-all-start.2 = ((bf16[128,16,128]{0,2,1:T(8,128)(2,1)}), bf16[128,16,128]{0,2,1:T(8,128)(2,1)}, u32[]{:S(2)}, u32[]{:S(2)}) async-start(bf16[128,16,128]{0,2,1:T(8,128)(2,1)} %bitcast.7), calls=%async_computation.2 | async-start | bytes 1048576 | tf_op jit(solution)/shard_map/all_to_all | solution.py:101
  83.3 221.0 %all-gather.4.cloned.1.call-start = ((), (), s32[]{:S(2)}) async-start(), calls=%async_computation.8 | async-start | bytes 2228224 | tf_op jit(solution)/shard_map/all_gather | solution.py:120
  83.5 1.4 copy-start.23
  83.6 3.1 copy-start.29
  83.9 1.5 copy-start.21
  84.3 3.7 copy-start.6
  84.9 1.3 copy-start.14
  102.9 2.8 copy-start.15
  104.2 1.5 copy-start.27
  104.2 2.3 copy-start.31
  106.5 2.2 copy-start
  139.2 26.3 %all-to-all-start.3 = ((bf16[128,16,128]{2,0,1:T(8,128)(2,1)}), bf16[128,16,128]{2,0,1:T(8,128)(2,1)}, u32[]{:S(2)}, u32[]{:S(2)}) async-start(bf16[128,16,128]{2,0,1:T(8,128)(2,1)} %bitcast.131), calls=%async_computation.3 | async-start | bytes 1048576 | tf_op jit(solution)/shard_map/all_to_all | solution.py:100
  165.5 43.7 %all-to-all-start.7 = ((bf16[128,16,256]{0,2,1:T(8,128)(2,1)}), bf16[128,16,256]{0,2,1:T(8,128)(2,1)}, u32[]{:S(2)}, u32[]{:S(2)}) async-start(bf16[128,16,256]{0,2,1:T(8,128)(2,1)} %bitcast.122), calls=%async_computation.7 | async-start | bytes 2097152 | tf_op jit(solution)/shard_map/all_to_all | solution.py:119
  174.8 246.2 %all-gather.6.cloned.1.call-start = ((), (), s32[]{:S(2)}) async-start(), calls=%async_computation.10 | async-start | bytes 4456448 | tf_op jit(solution)/shard_map/all_gather | solution.py:127
  175.5 4.4 copy-start.7
  175.5 4.4 copy-start.28
  179.9 1.1 copy-start.24
  180.3 0.8 copy-start.12
  181.4 1.6 copy-start.16
  181.5 1.6 copy-start.32
  183.7 0.9 copy-start.22
  183.8 2.6 copy-start.1
  184.6 1.0 copy-start.8
  188.9 1.2 copy-start.2
  190.8 3.4 copy-start.30
  192.8 1.4 copy-start.4
  194.2 28.0 %copy-start.13 = (bf16[512,512]{0,1:T(8,128)(2,1)S(1)}, bf16[512,512]{0,1:T(8,128)(2,1)}, u32[]{:S(2)}) copy-start(bf16[512,512]{0,1:T(8,128)(2,1)} %copy-done.12) | copy-start | bytes 1572868
  194.2 29.4 %copy-start.9 = (bf16[512,1024]{1,0:T(8,128)(2,1)S(1)}, bf16[512,1024]{1,0:T(8,128)(2,1)}, u32[]{:S(2)}) copy-start(bf16[512,1024]{1,0:T(8,128)(2,1)} %copy-done.8) | copy-start | bytes 3145732
  195.8 29.3 %copy-start.3 = (bf16[512,1536]{1,0:T(8,128)(2,1)S(1)}, bf16[512,1536]{1,0:T(8,128)(2,1)}, u32[]{:S(2)}) copy-start(bf16[512,1536]{1,0:T(8,128)(2,1)} %copy-done.2) | copy-start | bytes 4718596
  195.8 29.3 %copy-start.18 = (bf16[12,128,128]{2,1,0:T(8,128)(2,1)S(1)}, bf16[12,128,128]{2,1,0:T(8,128)(2,1)}, u32[]{:S(2)}) copy-start(bf16[12,128,128]{2,1,0:T(8,128)(2,1)} %copy-done.17) | copy-start | bytes 1179652
  209.2 67.0 %all-to-all-start.5 = ((bf16[16,128,128]{2,1,0:T(8,128)(2,1)}), bf16[16,128,128]{2,1,0:T(8,128)(2,1)}, u32[]{:S(2)}, u32[]{:S(2)}) async-start(bf16[16,128,128]{2,1,0:T(8,128)(2,1)} %bitcast.134), calls=%async_computation.5 | async-start | bytes 1048576 | tf_op jit(solution)/shard_map/all_to_all | solution.py:109
  222.2 3.4 copy-start.5
  222.2 3.4 copy-start.11
  276.2 26.7 %all-to-all-start.4 = ((bf16[16,128,128]{2,1,0:T(8,128)(2,1)}), bf16[16,128,128]{2,1,0:T(8,128)(2,1)S(1)}, u32[]{:S(2)}, u32[]{:S(2)}) async-start(bf16[16,128,128]{2,1,0:T(8,128)(2,1)} %bitcast.22), calls=%async_computation.4 | async-start | bytes 1048576 | tf_op jit(solution)/shard_map/all_to_all | solution.py:108
  280.5 260.3 %all-reduce.4.cloned.1.call-start = ((), (), s32[]{:S(2)}) async-start(), calls=%async_computation.9 | async-start | bytes 524288 | tf_op jit(solution)/shard_map/psum | solution.py:124
  304.2 116.7 %copy-start.19 = (bf16[128,4,128]{0,2,1:T(8,128)(2,1)S(1)}, bf16[128,4,128]{0,2,1:T(8,128)(2,1)}, u32[]{:S(2)}) copy-start(bf16[128,4,128]{0,2,1:T(8,128)(2,1)} %copy.65) | copy-start | bytes 393220
Sparse Core Ops, SparseCore 0:
  135.9 150.1 all-gather.3
  289.4 131.5 all-gather.5
  424.5 116.3 all-reduce.3
where the time goes:
time: 551 us; the launch traced here: 549 us
  waiting for transfers between devices  372 us (68%)
  starting transfers between devices  70.8 us (13%)
  matrix products  29.5 us (5%)
  local copies, waits for them, and re-layouts  29.1 us (5%)
  blocking collectives  23.9 us (4%)
  between operations  14.4 us (3%)
  other arithmetic  9.01 us (2%)
    psum x1, waiting for transfers between devices, local(): lax.psum(weight_term.astype(jnp.bfloat16), 'dp').astype(jnp.float32)  115 us
    all_gather x1, waiting for transfers between devices, local(): lax.all_gather(value_proj, 'seq', axis=0, tiled=True)  114 us
    all_to_all x1, waiting for transfers between devices, local(): lax.all_to_all(key_terms, 'seq', split_axis=0, concat_axis=1, tiled=True)  49 us
    all_to_all x1, blocking collectives, local(): lax.all_to_all(value_terms, 'seq', split_axis=0, concat_axis=1, tiled=True)  23.9 us
    all_to_all x1, waiting for transfers between devices, local(): lax.all_to_all(widen(key_rows), 'seq', split_axis=1, concat_axis=0, tiled...  19.1 us
    all_to_all x1, waiting for transfers between devices, local(): lax.all_to_all(query_terms, 'seq', split_axis=0, concat_axis=1, tiled=True)  18.8 us
    all_to_all x1, starting transfers between devices, local(): lax.all_to_all(widen(key_rows), 'seq', split_axis=1, concat_axis=0, tiled...  17.8 us
    all_to_all x1, waiting for transfers between devices, local(): lax.all_to_all(widen(value_rows), 'seq', split_axis=1, concat_axis=0, til...  17.4 us
  transfers between devices with their start and end apart: 11, of which 10 were waited for; matrix products, arithmetic and copies ran while one was open for 9% of the time, Pallas kernels for 0%

commit v1 on v0

v1 whole, which is shorter than its diff:
```python
import functools

import jax
import jax.numpy as jnp
from jax import lax
from jax.experimental import pallas as pl
from jax.experimental.pallas import tpu as pltpu
from jax.sharding import PartitionSpec as P

HEAD = 128
HQ = 16
CHUNK = 256
GROUP = 512
FACTOR = HEAD**-0.5
LOG2E = 1.4426950408889634
MASKED = -1e30
MESH = pl.DeviceIdType.MESH
F32 = jnp.float32
BF16 = jnp.bfloat16


def nt(a, b):
    return lax.dot_general(a, b, (((1,), (1,)), ((), ())), preferred_element_type=F32)


def nn(a, b):
    return lax.dot_general(a, b, (((1,), (0,)), ((), ())), preferred_element_type=F32)


def tn(a, b):
    return lax.dot_general(a, b, (((0,), (0,)), ((), ())), preferred_element_type=F32)


def aligned(index, size):
    return pl.ds(pl.multiple_of(index * size, size), size)


def fold8(x, op):
    return op(x.reshape(CHUNK // 8, 8, GROUP), axis=0)


def kernel(
    q_ref,
    k_ref,
    v_ref,
    g_ref,
    n_ref,
    w_ref,
    dq_o,
    dk_o,
    gn_o,
    dw_o,
    kbuf,
    vbuf,
    qbuf,
    ubuf,
    nbuf,
    wbuf,
    sbuf,
    ebuf,
    qs,
    us,
    stat,
    dvsend,
    dvown,
    dvsib,
    dvcs,
    dvcr,
    dksend,
    dkown,
    dksib,
    dkcs,
    dkcr,
    dvfull,
    dkfin,
    dqs,
    rsend,
    rown,
    rsib,
    rfull,
    zrecv,
    zfin,
    gns,
    send_sems,
    recv_sems,
):
    i = lax.axis_index("dp")
    x = lax.axis_index("pipe")
    s = lax.axis_index("seq")
    h = s // 8
    y = lax.rem(s // 2, 4)
    c = lax.rem(s, 2)
    z = h * 8 + i
    lower = h == 0
    upper = h == 1
    used = [0]
    started = []

    def rc(src, dst, dev):
        n = used[0]
        used[0] += 1
        return pltpu.make_async_remote_copy(
            src_ref=src,
            dst_ref=dst,
            send_sem=send_sems.at[n],
            recv_sem=recv_sems.at[n],
            device_id=dev,
            device_id_type=MESH,
        )

    def go(copy):
        copy.start()
        started.append(copy)

    def ydev(d):
        return {"seq": h * 8 + lax.rem(y + d, 4) * 2 + c}

    def zdev(d):
        t = lax.rem(z + d, 16)
        return {"dp": lax.rem(t, 8), "seq": (t // 8) * 8 + y * 2 + c}

    sib = {"seq": s + 1 - 2 * c}
    ys = [lax.rem(y + d, 4) for d in range(4)]
    yfrom = [lax.rem(y + 4 - d, 4) for d in range(4)]

    bar = pltpu.get_barrier_semaphore()
    count = 0
    for d in range(1, 4):
        pl.semaphore_signal(bar, inc=1, device_id=ydev(d), device_id_type=MESH)
        count += 1
    for d in range(4):
        pl.semaphore_signal(
            bar,
            inc=1,
            device_id={"pipe": lax.rem(x + 1, 4), "seq": ydev(d)["seq"]},
            device_id_type=MESH,
        )
        count += 1
    pl.semaphore_signal(bar, inc=1, device_id=sib, device_id_type=MESH)
    count += 1
    for d in range(1, 16):
        pl.semaphore_signal(bar, inc=1, device_id=zdev(d), device_id_type=MESH)
        count += 1
    pl.semaphore_wait(bar, count)

    my_rows = aligned(y, 128)
    kc = [
        rc(k_ref.at[:, aligned(ys[d], 128)], kbuf.at[0, c, my_rows], ydev(d)) for d in range(1, 4)
    ]
    for copy in kc:
        go(copy)
    kbuf[0, c, my_rows, :] = k_ref[:, my_rows]

    def crossing(buf):
        return [
            rc(buf.at[0, c, aligned(yfrom[d], 128)], buf.at[1, c, aligned(yfrom[d], 128)], zdev(8))
            for d in range(4)
        ]

    kx = crossing(kbuf)

    @pl.when(lower)
    def _():
        kx[0].start()

    qc = [
        rc(q_ref.at[:, aligned(ys[d], GROUP)], qbuf.at[y], ydev(d)) for d in range(1, 4)
    ]
    for copy in qc:
        go(copy)
    qbuf[y] = q_ref[:, aligned(y, GROUP)]
    vc = [
        rc(v_ref.at[:, aligned(ys[d], 128)], vbuf.at[0, c, my_rows], ydev(d)) for d in range(1, 4)
    ]
    for copy in vc:
        go(copy)
    vbuf[0, c, my_rows, :] = v_ref[:, my_rows]
    vx = crossing(vbuf)
    uc = [
        rc(
            g_ref.at[:, aligned(ys[d], GROUP)],
            ubuf.at[y],
            {"pipe": lax.rem(x + 3, 4), "seq": ydev(d)["seq"]},
        )
        for d in range(4)
    ]
    for copy in uc:
        go(copy)

    for d in range(1, 4):
        kc[d - 1].wait_recv()

        @pl.when(lower)
        def _():
            kx[d].start()

    ksib = rc(kbuf.at[0, c], kbuf.at[0, c], sib)
    go(ksib)
    for d in range(1, 4):
        qc[d - 1].wait_recv()
    for b in range(4):
        for hd in range(4):
            qs[b, hd * 128 : hd * 128 + 128, :] = qbuf[b, :, hd * 128 : hd * 128 + 128]

    @pl.when(lower)
    def _():
        vx[0].start()

    for d in range(1, 4):
        vc[d - 1].wait_recv()

        @pl.when(lower)
        def _():
            vx[d].start()

    vsib = rc(vbuf.at[0, c], vbuf.at[0, c], sib)
    go(vsib)

    wsib = rc(w_ref, wbuf.at[0, c], sib)
    go(wsib)
    wbuf[0, c] = w_ref[...]
    n = used[0]
    used[0] += 2

    def wcopy(src, which, d):
        return pltpu.make_async_remote_copy(
            src_ref=src,
            dst_ref=wbuf.at[1, c],
            send_sem=send_sems.at[n + which],
            recv_sem=recv_sems.at[n],
            device_id=zdev(d),
            device_id_type=MESH,
        )

    first_up = i == 7
    first_down = i == 0
    w_first = [wcopy(w_ref, 0, 15), wcopy(w_ref, 0, 1)]
    w_next = [wcopy(wbuf.at[1, c], 1, 1), wcopy(wbuf.at[1, c], 1, 15)]

    @pl.when(first_down)
    def _():
        w_first[0].start()

    @pl.when(first_up)
    def _():
        w_first[1].start()

    def forward_w(step):
        @pl.when(i == step)
        def _():
            w_first[0].wait_recv()
            w_next[0].start()

        @pl.when(i == 7 - step)
        def _():
            w_first[0].wait_recv()
            w_next[1].start()

    ksib.wait_recv()

    def kchunk(buf, half, j):
        rows = aligned(j, 128)
        return jnp.concatenate([buf[half, 0, rows, :], buf[half, 1, rows, :]], axis=0)

    for b in range(4):

        def body(j, top):
            sc = nt(kchunk(kbuf, 0, j), qs[b])
            sbuf[b, aligned(j, CHUNK), :] = sc
            return jnp.maximum(top, fold8(sc, jnp.max))

        top = lax.fori_loop(0, b, body, jnp.full((8, GROUP), MASKED, F32))
        sc = nt(kchunk(kbuf, 0, b), qs[b])
        key_pos = lax.broadcasted_iota(jnp.int32, (CHUNK, GROUP), 0)
        row_pos = lax.rem(lax.broadcasted_iota(jnp.int32, (CHUNK, GROUP), 1), 128) + c * 128
        sc = jnp.where(key_pos <= row_pos, sc, MASKED)
        sbuf[b, b * CHUNK : (b + 1) * CHUNK, :] = sc
        stat[b] = jnp.maximum(top, fold8(sc, jnp.max))

    for d in range(4):
        uc[d].wait_recv()
    nc = [
        rc(
            n_ref.at[:, aligned((h + r * (1 - 2 * h)) * 4 + ys[d], GROUP)],
            nbuf.at[r, my_rows],
            ydev(d),
        )
        for d in range(1, 4)
        for r in range(2)
    ]
    for copy in nc:
        go(copy)
    for r in range(2):
        nbuf[r, my_rows, :] = n_ref[:, aligned((h + r * (1 - 2 * h)) * 4 + y, GROUP)]
    vsib.wait_recv()
    forward_w(0)

    kxs = rc(kbuf.at[1, c], kbuf.at[1, c], sib)
    vxs = rc(vbuf.at[1, c], vbuf.at[1, c], sib)

    @pl.when(upper)
    def _():
        for d in range(4):
            kx[d].wait_recv()
        kxs.start()
        kxs.wait_recv()
        for b in range(4):

            def body(j, top):
                sc = nt(kchunk(kbuf, 1, j), qs[b])
                sbuf[b, aligned(j + 4, CHUNK), :] = sc
                return jnp.maximum(top, fold8(sc, jnp.max))

            stat[b] = lax.fori_loop(0, 4, body, stat[b])

    for b in range(4):
        shift = jnp.max(stat[b], axis=0, keepdims=True) * (FACTOR * LOG2E)

        def body(j, total):
            e = jnp.exp2(sbuf[b, aligned(j, CHUNK), :] * (FACTOR * LOG2E) - shift)
            ebuf[b, aligned(j, CHUNK), :] = e.astype(BF16)
            return total + fold8(e, jnp.sum)

        total = lax.fori_loop(0, b + 1, body, jnp.zeros((8, GROUP), F32))
        total = lax.fori_loop(4, 4 + 4 * h, body, total)
        inverse = 1.0 / jnp.sum(total, axis=0, keepdims=True)
        stat[b] = jnp.broadcast_to(inverse, (8, GROUP))
        for hd in range(4):
            cols = slice(hd * 128, hd * 128 + 128)
            spread = jnp.broadcast_to(inverse[:, cols], (128, 128)).T
            us[b, cols, :] = (ubuf[b, :, cols].astype(F32) * spread).astype(BF16)

    def split(term, own, send, rows):
        first, second = term[:128], term[128:]
        own[rows, :] = jnp.where(c == 0, first, second)
        send[rows, :] = jnp.where(c == 0, second, first).astype(BF16)

    def remote_terms(right, own, send):
        def body(j, carry):
            term = nn(ebuf[0, aligned(j + 4, CHUNK), :], right[0])
            for b in range(1, 4):
                term += nn(ebuf[b, aligned(j + 4, CHUNK), :], right[b])
            split(term, own, send, aligned(j, 128))
            return carry

        lax.fori_loop(0, 4, body, 0)

    def own_terms(right, own, send):
        for j in range(4):
            term = nn(ebuf[j, j * CHUNK : (j + 1) * CHUNK, :], right[j])
            for b in range(j + 1, 4):
                term += nn(ebuf[b, j * CHUNK : (j + 1) * CHUNK, :], right[b])
            split(term, own, send, slice(j * 128, j * 128 + 128))

    dvxs = rc(dvsend.at[1], dvsib.at[1], sib)
    dvos = rc(dvsend.at[0], dvsib.at[0], sib)
    dvx = rc(dvcs, dvcr, zdev(8))

    @pl.when(upper)
    def _():
        remote_terms(us, dvown.at[1], dvsend.at[1])
        dvxs.start()

    own_terms(us, dvown.at[0], dvsend.at[0])
    go(dvos)
    forward_w(1)

    @pl.when(upper)
    def _():
        dvxs.wait_recv()
        dvcs[...] = (dvown[1] + dvsib[1].astype(F32)).astype(BF16)
        dvx.start()

    my_head = aligned(y, 128)
    dvb = [rc(dvfull.at[:, my_head], dvfull.at[:, my_head], ydev(d)) for d in range(1, 4)]

    def send_dv():
        for copy in dvb:
            copy.start()

    dvos.wait_recv()

    @pl.when(upper)
    def _():
        dvfull[:, my_head] = (dvown[0] + dvsib[0].astype(F32)).astype(BF16)
        send_dv()
        for d in range(4):
            vx[d].wait_recv()
        vxs.start()
        vxs.wait_recv()

    for b in range(4):

        def body(j, total):
            half = j // 4
            dp = nt(kchunk(vbuf, half, lax.rem(j, 4)), us[b])
            t = ebuf[b, aligned(j, CHUNK), :].astype(F32) * dp
            sbuf[b, aligned(j, CHUNK), :] = t
            return total + fold8(t, jnp.sum)

        total = lax.fori_loop(0, b + 1, body, jnp.zeros((8, GROUP), F32))
        total = lax.fori_loop(4, 4 + 4 * h, body, total)
        inverse = stat[b]
        delta = jnp.sum(total, axis=0, keepdims=True) * inverse[0:1]

        def grads(j, carry):
            e = ebuf[b, aligned(j, CHUNK), :].astype(F32)
            ebuf[b, aligned(j, CHUNK), :] = (sbuf[b, aligned(j, CHUNK), :] - e * delta).astype(BF16)
            return carry

        lax.fori_loop(0, b + 1, grads, 0)
        lax.fori_loop(4, 4 + 4 * h, grads, 0)

    dkxs = rc(dksend.at[1], dksib.at[1], sib)
    dkos = rc(dksend.at[0], dksib.at[0], sib)
    dkx = rc(dkcs, dkcr, zdev(8))

    @pl.when(upper)
    def _():
        remote_terms(qs, dkown.at[1], dksend.at[1])
        dkxs.start()

    own_terms(qs, dkown.at[0], dksend.at[0])
    go(dkos)

    @pl.when(upper)
    def _():
        dkxs.wait_recv()
        dkcs[...] = ((dkown[1] + dksib[1].astype(F32)) * FACTOR).astype(BF16)
        dkx.start()

    forward_w(2)

    for b in range(4):

        def body(j, total):
            return total + tn(
                kchunk(kbuf, j // 4, lax.rem(j, 4)), ebuf[b, aligned(j, CHUNK), :]
            )

        total = lax.fori_loop(0, b + 1, body, jnp.zeros((HEAD, GROUP), F32))
        total = lax.fori_loop(4, 4 + 4 * h, body, total)
        total = total * FACTOR
        for hd in range(4):
            cols = slice(hd * 128, hd * 128 + 128)
            dqs[b, :, cols] = total[:, cols].T.astype(BF16)
    my_group = aligned(y, GROUP)
    dqc = [rc(dqs.at[ys[d]], dq_o.at[:, my_group], ydev(d)) for d in range(1, 4)]
    for copy in dqc:
        go(copy)
    dq_o[:, my_group] = dqs[y]

    dkos.wait_recv()
    dkc = [
        rc(dkfin.at[aligned(ys[d], 128)], dk_o.at[:, my_head], ydev(d)) for d in range(1, 4)
    ]

    def send_dk():
        for copy in dkc:
            copy.start()
        dk_o[:, my_head] = dkfin[my_rows, :]

    @pl.when(upper)
    def _():
        dkfin[...] = ((dkown[0] + dksib[0].astype(F32)) * FACTOR).astype(BF16)
        send_dk()

    @pl.when(lower)
    def _():
        dvx.wait_recv()
        dvfull[:, my_head] = (
            dvown[0] + dvsib[0].astype(F32) + dvcr[...].astype(F32)
        ).astype(BF16)
        send_dv()

    @pl.when(jnp.logical_or(i == 3, i == 4))
    def _():
        w_first[0].wait_recv()

    ws2 = rc(wbuf.at[1, c], wbuf.at[1, c], sib)
    go(ws2)
    for copy in nc:
        copy.wait_recv()
    for copy in dvb:
        copy.wait_recv()

    for r in range(2):
        rsend[r] = tn(nbuf[r, :, aligned(1 - c, CHUNK)], dvfull[...]).astype(BF16)
    rs = rc(rsend, rsib, sib)
    go(rs)
    for r in range(2):
        rown[r] = tn(nbuf[r, :, aligned(c, CHUNK)], dvfull[...])
    rs.wait_recv()
    for r in range(2):
        rfull[r] = (rown[r] + rsib[r].astype(F32)).astype(BF16)
    zc = []
    for d in range(1, 16):
        t = lax.rem(z + d, 16)
        r = lax.rem(t // 8 + h, 2)
        copy = rc(rfull.at[r, aligned(lax.rem(t, 8), 32)], zrecv.at[d - 1], zdev(d))
        zc.append(copy)
        go(copy)

    wsib.wait_recv()
    ws2.wait_recv()
    for r in range(2):
        for cc in range(2):
            gns[r, :, cc * CHUNK : (cc + 1) * CHUNK] = nt(dvfull[...], wbuf[r, cc]).astype(BF16)
    gc = []
    for r in range(2):
        cols = aligned((h + r * (1 - 2 * h)) * 4 + y, GROUP)
        for d in range(1, 4):
            copy = rc(gns.at[r, aligned(ys[d], 128)], gn_o.at[:, cols], ydev(d))
            gc.append(copy)
            go(copy)
        gn_o[:, cols] = gns[r, my_rows, :]

    @pl.when(lower)
    def _():
        dkx.wait_recv()
        dkfin[...] = (
            (dkown[0] + dksib[0].astype(F32)) * FACTOR + dkcr[...].astype(F32)
        ).astype(BF16)
        send_dk()

    my_piece = aligned(i, 32)
    total = rfull[0, my_piece, :].astype(F32)
    for d in range(15):
        zc[d].wait_recv()
        total += zrecv[d].astype(F32)
    zfin[my_piece, :] = total.astype(BF16)
    pc = [
        rc(zfin.at[my_piece], zfin.at[my_piece], {"dp": lax.rem(i + d, 8)}) for d in range(1, 8)
    ]
    for copy in pc:
        go(copy)
    for copy in pc:
        copy.wait_recv()
    dw_o[...] = zfin[...].astype(F32)

    for copy in dqc + dkc + gc:
        copy.wait_recv()
    for copy in started + dvb + dkc:
        copy.wait_send()

    @pl.when(lower)
    def _():
        for copy in kx + vx:
            copy.wait_send()

    @pl.when(upper)
    def _():
        for copy in [kxs, vxs, dvxs, dvx, dkxs, dkx]:
            copy.wait_send()

    @pl.when(jnp.logical_or(first_up, first_down))
    def _():
        w_first[0].wait_send()

    @pl.when(jnp.logical_and(i != 3, i != 4))
    def _():
        w_next[0].wait_send()


def local(queries, keys, values, grad_next, normed, value_weight):
    vmem = pl.BlockSpec(memory_space=pltpu.VMEM)

    def buf(*shape, dtype=BF16):
        return pltpu.VMEM(shape, dtype)

    count = 100
    dq, dk, gn, dw = pl.pallas_call(
        kernel,
        out_shape=(
            jax.ShapeDtypeStruct((128, 2048), BF16),
            jax.ShapeDtypeStruct((128, 512), BF16),
            jax.ShapeDtypeStruct((128, 4096), BF16),
            jax.ShapeDtypeStruct((256, 512), F32),
        ),
        in_specs=[vmem] * 6,
        out_specs=(vmem,) * 4,
        scratch_shapes=[
            buf(2, 2, 512, 128),
            buf(2, 2, 512, 128),
            buf(4, 128, GROUP),
            buf(4, 128, GROUP),
            buf(2, 512, GROUP),
            buf(2, 2, 256, 512),
            buf(4, 2048, GROUP, dtype=F32),
            buf(4, 2048, GROUP),
            buf(4, GROUP, HEAD),
            buf(4, GROUP, HEAD),
            buf(4, 8, GROUP, dtype=F32),
            buf(2, 512, 128),
            buf(2, 512, 128, dtype=F32),
            buf(2, 512, 128),
            buf(512, 128),
            buf(512, 128),
            buf(2, 512, 128),
            buf(2, 512, 128, dtype=F32),
            buf(2, 512, 128),
            buf(512, 128),
            buf(512, 128),
            buf(512, 512),
            buf(512, 128),
            buf(4, 128, GROUP),
            buf(2, 256, 512),
            buf(2, 256, 512, dtype=F32),
            buf(2, 256, 512),
            buf(2, 256, 512),
            buf(15, 32, 512),
            buf(256, 512),
            buf(2, 512, GROUP),
            pltpu.SemaphoreType.DMA((count,)),
            pltpu.SemaphoreType.DMA((count,)),
        ],
        compiler_params=pltpu.CompilerParams(
            collective_id=0, has_side_effects=True, vmem_limit_bytes=52 * 1024 * 1024
        ),
        cost_estimate=pl.CostEstimate(
            flops=6_000_000_000, bytes_accessed=5_000_000, transcendentals=3_000_000
        ),
    )(queries[0, 0], keys[0, 0], values[0, 0], grad_next[0, 0], normed[0, 0], value_weight[0])
    return dq[None, None], dk[None, None], gn[None, None], dw[None]


def solution(mesh):
    placed = (
        P("pipe", "dp", "seq", None),
        P("pipe", "dp", "seq", None),
        P("pipe", "dp", "seq", None),
        P("pipe", "dp", "seq", None),
        P("pipe", "dp", "seq", None),
        P("pipe", "seq", None),
    )
    return jax.shard_map(
        local,
        mesh=mesh,
        in_specs=placed,
        out_specs=(
            P("pipe", "dp", "seq", None),
            P("pipe", "dp", "seq", None),
            P("pipe", "dp", "seq", None),
            P("pipe", "seq", None),
        ),
        check_vma=False,
    )
```

time: 551 us -> 129 us (0.23)
  waiting for transfers between devices: 372 us -> 0 us
  Pallas kernels: 0 us -> 120 us
  starting transfers between devices: 70.8 us -> 0 us
  matrix products: 29.5 us -> 0 us
  blocking collectives: 23.9 us -> 0 us
  local copies, waits for them, and re-layouts: 29.1 us -> 5.97 us
  between operations: 14.4 us -> 0.66 us
  other arithmetic: 9.01 us -> 0 us
    all_to_all x7 -> x0, waiting for transfers between devices: 129 us -> none  [the longest x1 49 us: local(): lax.all_to_all(key_terms, 'seq', split_axis=0, concat_axis=1, tiled=True)]
    pallas_call x0 -> x1, Pallas kernels: none -> 120 us  [local(): pl.pallas_call(kernel, out_shape=(jax.ShapeDtypeStruct((128, 2048), BF16)...]
    psum x1 -> x0, waiting for transfers between devices: 115 us -> none  [local(): lax.psum(weight_term.astype(jnp.bfloat16), 'dp').astype(jnp.float32)]
    all_gather x2 -> x0, waiting for transfers between devices: 114 us -> none  [the longest x1 114 us: local(): lax.all_gather(value_proj, 'seq', axis=0, tiled=True)]
    all_to_all x7 -> x0, starting transfers between devices: 67.8 us -> none  [the longest x1 17.8 us: local(): lax.all_to_all(widen(key_rows), 'seq', split_axis=1, concat_axis=0, tiled...]
    dot_general x26 -> x0, matrix products: 29.5 us -> none  [the longest x1 4.65 us: local(): lax.dot_general(value_grad_rows, lax.all_gather(value_proj, 'seq', axis=0...]
    all_to_all x1 -> x0, blocking collectives: 23.9 us -> none  [local(): lax.all_to_all(value_terms, 'seq', split_axis=0, concat_axis=1, tiled=True)]
    ppermute x1 -> x0, waiting for transfers between devices: 14.4 us -> none  [passed_along(): return lax.ppermute(block, axis, route)]
  transfers between devices with their start and end apart: 11 -> 0, of which waited for: 10 -> 0; matrix products, arithmetic and copies ran while one was open for 9% -> 0% of each run, Pallas kernels for 0% -> 0%
where the time goes in v1:
time: 129 us; the launch traced here: 127 us
  Pallas kernels  120 us (93%)
  local copies, waits for them, and re-layouts  5.97 us (5%)
    pallas_call x1, Pallas kernels, local(): pl.pallas_call(kernel, out_shape=(jax.ShapeDtypeStruct((128, 2048), BF16)...  120 us
    unnamed x12, local copies, waits for them, and re-layouts  5.97 us

profile of v1, /device:TPU:6, one launch (start us, length us, event | category | flops | bytes accessed | tf_op | source)
XLA Modules:
  0.0 126.8 jit_solution(14444782352358397148)
XLA Ops:
  0.6 0.0 copy-start
  0.6 0.9 copy-done
  1.6 0.0 copy-start.1
  1.6 0.9 copy-done.1
  2.5 0.0 copy-start.2
  2.5 0.9 copy-done.2
  3.4 120.1 %shard_map.93 = (bf16[128,2048]{1,0:T(8,128)(2,1)S(1)}, bf16[128,512]{1,0:T(8,128)(2,1)S(1)}, bf16[128,4096]{1,0:T(8,128)(2,1)}, f32[256,512]{1,0:T(8,128)S(1)}) custom-call(bf16[128,2048]{1,0:T(8,128)(2,1)} %bitcast.18, bf16[128,512]{1,0:T(8,128)(2,1)S(1)} %bitcast.14, bf16[128,512]{1,0:T(8,128)(2,1)S(1)} %bitcast.15, bf16[128,2048]{1,0:T(8,128)(2,1)} %bitcast.19, ...), custom_call_target="tpu_custom_call" | custom-call | flops 6000000000 | bytes 5000000 | tf_op jit(solution)/shard_map/pallas_call | solution.py:572
  123.5 0.0 copy-start.3
  123.5 0.8 copy.14
  124.3 0.7 copy.15
  125.0 0.0 copy-done.3
  125.0 1.0 copy.16
  126.0 0.8 copy.17
Async XLA Ops:
  0.6 1.0 copy-start
  1.6 0.9 copy-start.1
  2.5 0.9 copy-start.2
  123.5 1.5 %copy-start.3 = (bf16[128,4096]{1,0:T(8,128)(2,1)S(1)}, bf16[128,4096]{1,0:T(8,128)(2,1)}, u32[]{:S(2)}) copy-start(bf16[128,4096]{1,0:T(8,128)(2,1)} %get-tuple-element.10) | copy-start | bytes 3145732

commit v2 on v1

v2 whole, which is shorter than its diff:
```python
import functools

import jax
import jax.numpy as jnp
from jax import lax
from jax.experimental import pallas as pl
from jax.experimental.pallas import tpu as pltpu
from jax.sharding import PartitionSpec as P

HEAD = 128
HQ = 16
CHUNK = 256
GROUP = 512
FACTOR = HEAD**-0.5
LOG2E = 1.4426950408889634
MASKED = -1e30
MESH = pl.DeviceIdType.MESH
F32 = jnp.float32
BF16 = jnp.bfloat16


def nt(a, b):
    return lax.dot_general(a, b, (((1,), (1,)), ((), ())), preferred_element_type=F32)


def nn(a, b):
    return lax.dot_general(a, b, (((1,), (0,)), ((), ())), preferred_element_type=F32)


def tn(a, b):
    return lax.dot_general(a, b, (((0,), (0,)), ((), ())), preferred_element_type=F32)


def aligned(index, size):
    return pl.ds(pl.multiple_of(index * size, size), size)


def fold8(x, op):
    return op(x.reshape(CHUNK // 8, 8, GROUP), axis=0)


def kernel(
    q_ref,
    k_ref,
    v_ref,
    g_ref,
    n_ref,
    w_ref,
    dq_o,
    dk_o,
    gn_o,
    dw_o,
    kbuf,
    vbuf,
    qbuf,
    ubuf,
    nbuf,
    wbuf,
    sbuf,
    ebuf,
    qs,
    ust,
    kt,
    vt,
    stat,
    dvsend,
    dvown,
    dvsib,
    dvcs,
    dvcr,
    dksend,
    dkown,
    dksib,
    dkcs,
    dkcr,
    dvfull,
    dkfin,
    dqs,
    rsend,
    rsib,
    rfull,
    z1recv,
    tfull,
    z2recv,
    zfin,
    gns,
    send_sems,
    recv_sems,
    local_sems,
):
    i = lax.axis_index("dp")
    x = lax.axis_index("pipe")
    s = lax.axis_index("seq")
    h = s // 8
    y = lax.rem(s // 2, 4)
    c = lax.rem(s, 2)
    z = h * 8 + i
    lower = h == 0
    upper = h == 1
    used = [0]
    local_used = [0]
    started = []

    def lc(src, dst):
        n = local_used[0]
        local_used[0] += 1
        return pltpu.make_async_copy(src, dst, local_sems.at[n])

    def rc(src, dst, dev):
        n = used[0]
        used[0] += 1
        return pltpu.make_async_remote_copy(
            src_ref=src,
            dst_ref=dst,
            send_sem=send_sems.at[n],
            recv_sem=recv_sems.at[n],
            device_id=dev,
            device_id_type=MESH,
        )

    def go(copy):
        copy.start()
        started.append(copy)

    def ydev(d):
        return {"seq": h * 8 + lax.rem(y + d, 4) * 2 + c}

    def zdev(d):
        t = lax.rem(z + d, 16)
        return {"dp": lax.rem(t, 8), "seq": (t // 8) * 8 + y * 2 + c}

    sib = {"seq": s + 1 - 2 * c}
    ys = [lax.rem(y + d, 4) for d in range(4)]
    yfrom = [lax.rem(y + 4 - d, 4) for d in range(4)]

    bar = pltpu.get_barrier_semaphore()
    count = 0
    for d in range(1, 4):
        pl.semaphore_signal(bar, inc=1, device_id=ydev(d), device_id_type=MESH)
        count += 1
    for d in range(4):
        pl.semaphore_signal(
            bar,
            inc=1,
            device_id={"pipe": lax.rem(x + 1, 4), "seq": ydev(d)["seq"]},
            device_id_type=MESH,
        )
        count += 1
    pl.semaphore_signal(bar, inc=1, device_id=sib, device_id_type=MESH)
    count += 1
    for d in range(1, 8):
        dev = {"dp": lax.rem(i + d, 8)}
        pl.semaphore_signal(bar, inc=1, device_id=dev, device_id_type=MESH)
        count += 1
    for d in (1, 4, 8, 12, 15):
        pl.semaphore_signal(bar, inc=1, device_id=zdev(d), device_id_type=MESH)
        count += 1
    my_rows = aligned(y, 128)
    my_group = aligned(y, GROUP)
    column_blocks = [lax.rem(h + r, 2) * 4 for r in range(2)]
    own_k = lc(k_ref.at[:, my_rows], kbuf.at[0, c, my_rows])
    own_q = lc(q_ref.at[:, my_group], qbuf.at[y])
    own_v = lc(v_ref.at[:, my_rows], vbuf.at[0, c, my_rows])
    own_w = lc(w_ref, wbuf.at[0, c])
    own_n = [
        lc(n_ref.at[:, aligned(column_blocks[r] + y, GROUP)], nbuf.at[r, my_rows])
        for r in range(2)
    ]
    for copy in [own_k, own_q, own_v, own_w] + own_n:
        copy.start()
    pl.semaphore_wait(bar, count)

    kc = [
        rc(k_ref.at[:, aligned(ys[d], 128)], kbuf.at[0, c, my_rows], ydev(d)) for d in range(1, 4)
    ]
    for copy in kc:
        go(copy)

    def crossing(ref, buf):
        copies = []
        for d in range(4):
            rows = aligned(yfrom[d], 128)
            src = ref.at[:, my_rows] if d == 0 else buf.at[0, c, rows]
            copies.append(rc(src, buf.at[1, c, rows], zdev(8)))
        return copies

    kx = crossing(k_ref, kbuf)

    @pl.when(lower)
    def _():
        kx[0].start()

    qc = [
        rc(q_ref.at[:, aligned(ys[d], GROUP)], qbuf.at[y], ydev(d)) for d in range(1, 4)
    ]
    for copy in qc:
        go(copy)
    vx = crossing(v_ref, vbuf)
    uc = [
        rc(
            g_ref.at[:, aligned(ys[d], GROUP)],
            ubuf.at[y],
            {"pipe": lax.rem(x + 3, 4), "seq": ydev(d)["seq"]},
        )
        for d in range(4)
    ]
    for copy in uc:
        go(copy)

    for d in range(1, 4):
        kc[d - 1].wait_recv()

        @pl.when(lower)
        def _():
            kx[d].start()

    own_k.wait()
    ksib = rc(kbuf.at[0, c], kbuf.at[0, c], sib)
    go(ksib)
    for d in range(1, 4):
        qc[d - 1].wait_recv()
    own_q.wait()
    vc = [
        rc(v_ref.at[:, aligned(ys[d], 128)], vbuf.at[0, c, my_rows], ydev(d)) for d in range(1, 4)
    ]
    for copy in vc:
        go(copy)
    for b in range(4):
        for hd in range(4):
            qs[b, hd * 128 : hd * 128 + 128, :] = qbuf[b, :, hd * 128 : hd * 128 + 128]


    wsib = rc(w_ref, wbuf.at[0, c], sib)
    go(wsib)
    n = used[0]
    used[0] += 2

    def wcopy(src, which, d):
        return pltpu.make_async_remote_copy(
            src_ref=src,
            dst_ref=wbuf.at[1, c],
            send_sem=send_sems.at[n + which],
            recv_sem=recv_sems.at[n],
            device_id=zdev(d),
            device_id_type=MESH,
        )

    first_up = i == 7
    first_down = i == 0

    def start_w():
        @pl.when(first_down)
        def _():
            w_first[0].start()

        @pl.when(first_up)
        def _():
            w_first[1].start()

    w_first = [wcopy(w_ref, 0, 15), wcopy(w_ref, 0, 1)]
    w_next = [wcopy(wbuf.at[1, c], 1, 1), wcopy(wbuf.at[1, c], 1, 15)]

    @pl.when(upper)
    def _():
        start_w()

    def forward_w(half, step):
        @pl.when(jnp.logical_and(half, i == step))
        def _():
            w_first[0].wait_recv()
            w_next[0].start()

        @pl.when(jnp.logical_and(half, i == 7 - step))
        def _():
            w_first[0].wait_recv()
            w_next[1].start()

    ksib.wait_recv()

    def kchunk(buf, half, j):
        rows = aligned(j, 128)
        return jnp.concatenate([buf[half, 0, rows, :], buf[half, 1, rows, :]], axis=0)

    for b in range(4):

        def body(j, top):
            sc = nt(kchunk(kbuf, 0, j), qs[b])
            sbuf[b, aligned(j, CHUNK), :] = sc
            return jnp.maximum(top, fold8(sc, jnp.max))

        top = lax.fori_loop(0, b, body, jnp.full((8, GROUP), MASKED, F32))
        sc = nt(kchunk(kbuf, 0, b), qs[b])
        key_pos = lax.broadcasted_iota(jnp.int32, (CHUNK, GROUP), 0)
        row_pos = lax.rem(lax.broadcasted_iota(jnp.int32, (CHUNK, GROUP), 1), 128) + c * 128
        sc = jnp.where(key_pos <= row_pos, sc, MASKED)
        sbuf[b, b * CHUNK : (b + 1) * CHUNK, :] = sc
        stat[b] = jnp.maximum(top, fold8(sc, jnp.max))

    for copy in vc:
        copy.wait_recv()
    own_v.wait()
    vsib = rc(vbuf.at[0, c], vbuf.at[0, c], sib)
    go(vsib)

    @pl.when(lower)
    def _():
        for copy in kx:
            copy.wait_send()
        for copy in vx:
            copy.start()

    for d in range(4):
        uc[d].wait_recv()
    nc = [
        rc(
            n_ref.at[:, aligned(column_blocks[r] + ys[d], GROUP)],
            nbuf.at[r, my_rows],
            ydev(d),
        )
        for d in range(1, 4)
        for r in range(2)
    ]
    for copy in nc:
        go(copy)
    for b in range(4):
        for hd in range(4):
            cols = slice(hd * 128, hd * 128 + 128)
            ust[b, :, cols] = ubuf[b, :, cols].T
        kt[0, :, b * CHUNK : (b + 1) * CHUNK] = kchunk(kbuf, 0, b).T
    vsib.wait_recv()
    for b in range(4):
        vt[0, :, b * CHUNK : (b + 1) * CHUNK] = kchunk(vbuf, 0, b).T

    def across(buf):
        rows = [aligned(yfrom[d], 128) for d in range(4)]
        return [rc(buf.at[1, c, r], buf.at[1, c, r], sib) for r in rows]

    kxs = across(kbuf)
    vxs = rc(vbuf.at[1, c], vbuf.at[1, c], sib)

    @pl.when(upper)
    def _():
        for d in range(4):
            kx[d].wait_recv()
            kxs[d].start()
            kxs[d].wait_recv()
            part = kchunk(kbuf, 1, yfrom[d])
            kt[1, :, aligned(yfrom[d], CHUNK)] = part.T

            def body(b, carry):
                sc = nt(part, qs[b])
                sbuf[b, aligned(yfrom[d] + 4, CHUNK), :] = sc
                stat[b] = jnp.maximum(stat[b], fold8(sc, jnp.max))
                return carry

            lax.fori_loop(0, 4, body, 0)

    for b in range(4):
        shift = jnp.max(stat[b], axis=0, keepdims=True) * (FACTOR * LOG2E)

        def body(j, total):
            e = jnp.exp2(sbuf[b, aligned(j, CHUNK), :] * (FACTOR * LOG2E) - shift)
            ebuf[b, aligned(j, CHUNK), :] = e.astype(BF16)
            return total + fold8(e, jnp.sum)

        total = lax.fori_loop(0, b + 1, body, jnp.zeros((8, GROUP), F32))
        total = lax.fori_loop(4, 4 + 4 * h, body, total)
        inverse = 1.0 / jnp.sum(total, axis=0, keepdims=True)
        stat[b] = jnp.broadcast_to(inverse, (8, GROUP))
        ust[b] = (ust[b].astype(F32) * inverse).astype(BF16)

    def split(term, own, send, rows):
        first, second = term[:128], term[128:]
        own[rows, :] = jnp.where(c == 0, first, second)
        send[rows, :] = jnp.where(c == 0, second, first).astype(BF16)

    def remote_terms(product, right, own, send):
        def body(j, carry):
            term = product(ebuf[0, aligned(j + 4, CHUNK), :], right[0])
            for b in range(1, 4):
                term += product(ebuf[b, aligned(j + 4, CHUNK), :], right[b])
            split(term, own, send, aligned(j, 128))
            return carry

        lax.fori_loop(0, 4, body, 0)

    def own_terms(product, right, own, send):
        for j in range(4):
            term = product(ebuf[j, j * CHUNK : (j + 1) * CHUNK, :], right[j])
            for b in range(j + 1, 4):
                term += product(ebuf[b, j * CHUNK : (j + 1) * CHUNK, :], right[b])
            split(term, own, send, slice(j * 128, j * 128 + 128))

    dvxs = rc(dvsend.at[1], dvsib.at[1], sib)
    dvos = rc(dvsend.at[0], dvsib.at[0], sib)
    forward_w(lower, 0)
    block_rows = [slice(b * 128, b * 128 + 128) for b in range(4)]
    dvx = [rc(dvcs.at[r], dvcr.at[r], zdev(8)) for r in block_rows]

    @pl.when(upper)
    def _():
        remote_terms(nt, ust, dvown.at[1], dvsend.at[1])
        dvxs.start()

    own_terms(nt, ust, dvown.at[0], dvsend.at[0])
    go(dvos)
    forward_w(lower, 1)

    @pl.when(upper)
    def _():
        dvxs.wait_recv()
        dvcs[...] = (dvown[1] + dvsib[1].astype(F32)).astype(BF16)
        for copy in dvx:
            copy.start()

    my_head = aligned(y, 128)
    dvb = [
        [rc(dvfull.at[r, my_head], dvfull.at[r, my_head], ydev(d)) for d in range(1, 4)]
        for r in block_rows
    ]

    dvos.wait_recv()

    @pl.when(upper)
    def _():
        dvfull[:, my_head] = (dvown[0] + dvsib[0].astype(F32)).astype(BF16)
        for copies in dvb:
            for copy in copies:
                copy.start()
        for d in range(4):
            vx[d].wait_recv()
        vxs.start()
        vxs.wait_recv()
        for j in range(4):
            vt[1, :, j * CHUNK : (j + 1) * CHUNK] = kchunk(vbuf, 1, j).T

    forward_w(upper, 0)

    def by_keys(t, b):
        def far(_, total):
            return total + nn(t[1], ebuf[b, 1024:2048, :])

        near = nn(t[0, :, : (b + 1) * CHUNK], ebuf[b, : (b + 1) * CHUNK, :])
        return lax.fori_loop(0, h, far, near)

    for b in range(4):
        out = by_keys(vt, b)
        delta = jnp.sum(ust[b].astype(F32) * out, axis=0, keepdims=True) * stat[b, 0:1, :]

        def grads(j, carry):
            dp = nn(kchunk(vbuf, j // 4, lax.rem(j, 4)), ust[b])
            e = ebuf[b, aligned(j, CHUNK), :].astype(F32)
            ebuf[b, aligned(j, CHUNK), :] = (e * (dp - delta)).astype(BF16)
            return carry

        lax.fori_loop(0, b + 1, grads, 0)
        lax.fori_loop(4, 4 + 4 * h, grads, 0)

    dkxs = rc(dksend.at[1], dksib.at[1], sib)
    dkos = rc(dksend.at[0], dksib.at[0], sib)
    dkx = rc(dkcs, dkcr, zdev(8))

    @pl.when(upper)
    def _():
        remote_terms(nn, qs, dkown.at[1], dksend.at[1])
        dkxs.start()

    own_terms(nn, qs, dkown.at[0], dksend.at[0])
    go(dkos)

    forward_w(lower, 2)
    forward_w(upper, 1)

    def weight_grad():
        for copy in nc:
            copy.wait_recv()
        for copy in own_n:
            copy.wait()
        for copies in dvb:
            for copy in copies:
                copy.wait_recv()
        for r in (1, 0):
            rsend[r] = tn(nbuf[r, :, aligned(1 - c, CHUNK)], dvfull[...]).astype(BF16)
            rs[r].start()
        for r in (1, 0):
            rown = tn(nbuf[r, :, aligned(c, CHUNK)], dvfull[...])
            rs[r].wait_recv()
            total = (rown + rsib[r].astype(F32)).astype(BF16)
            for p in range(8):
                row = pl.multiple_of(column_blocks[r] * 16 + p // 4 * 32, 32)
                rfull[p % 4, pl.ds(row, 32), :] = total[p * 32 : p * 32 + 32]
            for copy in z1[r]:
                copy.start()

    rs = [rc(rsend.at[r], rsib.at[r], sib) for r in range(2)]
    za, zb = z // 4, lax.rem(z, 4)

    def group_dev(d):
        t = za * 4 + lax.rem(zb + d, 4)
        return {"dp": lax.rem(t, 8)}

    z_rows = [pl.ds(pl.multiple_of(column_blocks[r] * 16, 64), 64) for r in range(2)]
    z1 = [
        [
            rc(
                rfull.at[lax.rem(zb + d, 4), z_rows[r]],
                z1recv.at[d - 1, z_rows[r]],
                group_dev(d),
            )
            for d in range(1, 4)
        ]
        for r in range(2)
    ]

    for b in range(4):
        total = by_keys(kt, b)
        total = total * FACTOR
        for hd in range(4):
            cols = slice(hd * 128, hd * 128 + 128)
            dqs[b, :, cols] = total[:, cols].T.astype(BF16)
    dqc = [rc(dqs.at[ys[d]], dq_o.at[:, my_group], ydev(d)) for d in range(1, 4)]
    for copy in dqc:
        go(copy)
    out_dq = lc(dqs.at[y], dq_o.at[:, my_group])
    out_dq.start()

    @pl.when(upper)
    def _():
        for copy in dvx:
            copy.wait_send()
        dkxs.wait_recv()
        dkcs[...] = ((dkown[1] + dksib[1].astype(F32)) * FACTOR).astype(BF16)
        dkx.start()

    @pl.when(upper)
    def _():
        weight_grad()

    dkos.wait_recv()
    dkc = [
        rc(dkfin.at[aligned(ys[d], 128)], dk_o.at[:, my_head], ydev(d)) for d in range(1, 4)
    ]

    out_dk = lc(dkfin.at[my_rows], dk_o.at[:, my_head])

    def send_dk():
        for copy in dkc:
            copy.start()
        out_dk.start()

    @pl.when(upper)
    def _():
        dkfin[...] = ((dkown[0] + dksib[0].astype(F32)) * FACTOR).astype(BF16)
        send_dk()

    @pl.when(lower)
    def _():
        start_w()
        for b in range(4):
            dvx[b].wait_recv()
            r = block_rows[b]
            dvfull[r, my_head] = (
                dvown[0, r, :] + dvsib[0, r, :].astype(F32) + dvcr[r, :].astype(F32)
            ).astype(BF16)
            for copy in dvb[b]:
                copy.start()
        weight_grad()

    forward_w(upper, 2)
    @pl.when(jnp.logical_or(i == 3, i == 4))
    def _():
        w_first[0].wait_recv()

    ws2 = rc(wbuf.at[1, c], wbuf.at[1, c], sib)
    go(ws2)
    def z2copy(target, slot):
        dev = {"dp": target % 2 * 4 + zb, "seq": target // 2 * 8 + y * 2 + c}
        return rc(tfull.at[aligned(target, 32)], z2recv.at[slot], dev)

    other = [(1 - h) * 2 + lax.rem(za + e, 2) for e in range(2)]
    near = za + 1 - 2 * lax.rem(za, 2)
    z2 = [[z2copy(near, 0)], [z2copy(other[0], 1), z2copy(other[1], 2)]]
    for r in (1, 0):
        for copy in z1[r]:
            copy.wait_recv()
        total = rfull[zb, z_rows[r], :].astype(F32)
        for d in range(3):
            total += z1recv[d, z_rows[r], :].astype(F32)
        tfull[z_rows[r], :] = total.astype(BF16)
        for copy in z2[r]:
            go(copy)

    wsib.wait_recv()
    own_w.wait()
    ws2.wait_recv()
    for r in range(2):
        for cc in range(2):
            gns[r, :, cc * CHUNK : (cc + 1) * CHUNK] = nt(dvfull[...], wbuf[r, cc]).astype(BF16)
    gc = []
    out_gn = []
    for r in range(2):
        cols = aligned(column_blocks[r] + y, GROUP)
        for d in range(1, 4):
            copy = rc(gns.at[r, aligned(ys[d], 128)], gn_o.at[:, cols], ydev(d))
            gc.append(copy)
            go(copy)
        out_gn.append(lc(gns.at[r, my_rows], gn_o.at[:, cols]))
        out_gn[r].start()

    @pl.when(lower)
    def _():
        dkx.wait_recv()
        dkfin[...] = (
            (dkown[0] + dksib[0].astype(F32)) * FACTOR + dkcr[...].astype(F32)
        ).astype(BF16)
        send_dk()

    my_piece = aligned(i, 32)
    total = tfull[aligned(za, 32), :].astype(F32)
    for copy in z2[0] + z2[1]:
        copy.wait_recv()
    for d in range(3):
        total += z2recv[d].astype(F32)
    zfin[my_piece, :] = total.astype(BF16)
    far_piece = aligned(lax.rem(i + 4, 8), 32)
    p1 = rc(zfin.at[my_piece], zfin.at[my_piece], {"dp": lax.rem(i + 4, 8)})
    go(p1)
    pc = [rc(zfin.at[my_piece], dw_o.at[my_piece], group_dev(d)) for d in range(1, 4)]
    for copy in pc:
        go(copy)
    p1.wait_recv()
    pf = [rc(zfin.at[far_piece], dw_o.at[far_piece], group_dev(d)) for d in range(1, 4)]
    for copy in pf:
        go(copy)
    out_dw = [lc(zfin.at[p], dw_o.at[p]) for p in (my_piece, far_piece)]
    for copy in out_dw:
        copy.start()
    for copy in pc + pf:
        copy.wait_recv()

    for copy in [out_dq, out_dk] + out_dw + out_gn:
        copy.wait()
    for copy in dqc + dkc + gc:
        copy.wait_recv()
    for copy in started + dkc + rs + [copy for copies in dvb + z1 for copy in copies]:
        copy.wait_send()

    @pl.when(lower)
    def _():
        for copy in vx:
            copy.wait_send()

    @pl.when(upper)
    def _():
        for copy in kxs + [vxs, dvxs, dkxs, dkx]:
            copy.wait_send()

    @pl.when(jnp.logical_or(first_up, first_down))
    def _():
        w_first[0].wait_send()

    @pl.when(jnp.logical_and(i != 3, i != 4))
    def _():
        w_next[0].wait_send()


def local(queries, keys, values, grad_next, normed, value_weight):
    anywhere = pl.BlockSpec(memory_space=pl.ANY)

    def buf(*shape, dtype=BF16):
        return pltpu.VMEM(shape, dtype)

    count = 100
    dq, dk, gn, dw = pl.pallas_call(
        kernel,
        out_shape=(
            jax.ShapeDtypeStruct((128, 2048), BF16),
            jax.ShapeDtypeStruct((128, 512), BF16),
            jax.ShapeDtypeStruct((128, 4096), BF16),
            jax.ShapeDtypeStruct((256, 512), BF16),
        ),
        in_specs=[anywhere] * 6,
        out_specs=(anywhere,) * 4,
        scratch_shapes=[
            buf(2, 2, 512, 128),
            buf(2, 2, 512, 128),
            buf(4, 128, GROUP),
            buf(4, 128, GROUP),
            buf(2, 512, GROUP),
            buf(2, 2, 256, 512),
            buf(4, 2048, GROUP, dtype=F32),
            buf(4, 2048, GROUP),
            buf(4, GROUP, HEAD),
            buf(4, HEAD, GROUP),
            buf(2, HEAD, 1024),
            buf(2, HEAD, 1024),
            buf(4, 8, GROUP, dtype=F32),
            buf(2, 512, 128),
            buf(2, 512, 128, dtype=F32),
            buf(2, 512, 128),
            buf(512, 128),
            buf(512, 128),
            buf(2, 512, 128),
            buf(2, 512, 128, dtype=F32),
            buf(2, 512, 128),
            buf(512, 128),
            buf(512, 128),
            buf(512, 512),
            buf(512, 128),
            buf(4, 128, GROUP),
            buf(2, 256, 512),
            buf(2, 256, 512),
            buf(4, 128, 512),
            buf(3, 128, 512),
            buf(128, 512),
            buf(3, 32, 512),
            buf(256, 512),
            buf(2, 512, GROUP),
            pltpu.SemaphoreType.DMA((count,)),
            pltpu.SemaphoreType.DMA((count,)),
            pltpu.SemaphoreType.DMA((16,)),
        ],
        compiler_params=pltpu.CompilerParams(
            collective_id=0, has_side_effects=True, vmem_limit_bytes=60 * 1024 * 1024
        ),
        cost_estimate=pl.CostEstimate(
            flops=6_000_000_000, bytes_accessed=5_000_000, transcendentals=3_000_000
        ),
    )(queries[0, 0], keys[0, 0], values[0, 0], grad_next[0, 0], normed[0, 0], value_weight[0])
    return dq[None, None], dk[None, None], gn[None, None], dw.astype(F32)[None]


def solution(mesh):
    placed = (
        P("pipe", "dp", "seq", None),
        P("pipe", "dp", "seq", None),
        P("pipe", "dp", "seq", None),
        P("pipe", "dp", "seq", None),
        P("pipe", "dp", "seq", None),
        P("pipe", "seq", None),
    )
    return jax.shard_map(
        local,
        mesh=mesh,
        in_specs=placed,
        out_specs=(
            P("pipe", "dp", "seq", None),
            P("pipe", "dp", "seq", None),
            P("pipe", "dp", "seq", None),
            P("pipe", "seq", None),
        ),
        check_vma=False,
    )
```

time: 129 us -> 114 us (0.88); the launches traced: 127 us -> 113 us
  Pallas kernels: 120 us -> 108 us
  local copies, waits for them, and re-layouts: 5.97 us -> 2.66 us
  other arithmetic: 0 us -> 1.92 us
    pallas_call x1, Pallas kernels: 120 us -> 108 us  [local(): pl.pallas_call(kernel, out_shape=(jax.ShapeDtypeStruct((128, 2048), BF16)...]
    unnamed x12 -> x9, local copies, waits for them, and re-layouts: 5.97 us -> 2.66 us
    broadcast_in_dim x0 -> x1, other arithmetic: none -> 1.92 us  [local(): dw.astype(F32)[None]]
where the time goes in v2:
time: 114 us; the launch traced here: 113 us
  Pallas kernels  108 us (95%)
  local copies, waits for them, and re-layouts  2.66 us (2%)
  other arithmetic  1.92 us (2%)
    pallas_call x1, Pallas kernels, local(): pl.pallas_call(kernel, out_shape=(jax.ShapeDtypeStruct((128, 2048), BF16)...  108 us
    unnamed x9, local copies, waits for them, and re-layouts  2.66 us

profile of v2, /device:TPU:6, one launch (start us, length us, event | category | flops | bytes accessed | tf_op | source)
XLA Modules:
  0.0 113.2 jit_solution(5295501104800804581)
XLA Ops:
  0.6 107.9 %shard_map.93 = (bf16[128,2048]{1,0:T(8,128)(2,1)}, bf16[128,512]{1,0:T(8,128)(2,1)}, bf16[128,4096]{1,0:T(8,128)(2,1)}, bf16[256,512]{1,0:T(8,128)(2,1)}) custom-call(bf16[128,2048]{1,0:T(8,128)(2,1)} %bitcast.16, bf16[128,512]{1,0:T(8,128)(2,1)} %bitcast.19, bf16[128,512]{1,0:T(8,128)(2,1)} %bitcast.20, bf16[128,2048]{1,0:T(8,128)(2,1)} %bitcast.17, ...), custom_call_target="tpu_custom_call" | custom-call | flops 6000000000 | bytes 5000000 | tf_op jit(solution)/shard_map/pallas_call | solution.py:674
  108.6 0.0 copy-start.1
  108.6 0.0 copy-start
  108.6 1.9 %bitcast_convert_fusion = f32[1,256,512]{2,1,0:T(8,128)} fusion(bf16[256,512]{1,0:T(8,128)(2,1)} %get-tuple-element.11), kind=kLoop, calls=%fused_computation | loop fusion | flops 131072 | bytes 786432 | tf_op jit(solution)/shard_map/broadcast_in_dim | solution.py:730
  110.5 0.0 copy-done.1
  110.5 0.0 copy-start.2
  110.5 0.8 copy.13
  111.3 0.2 copy-done.2
  111.5 0.7 copy.14
  112.2 0.0 copy-done
  112.2 1.0 copy.15
Async XLA Ops:
  108.6 1.9 %copy-start.1 = (bf16[128,2048]{1,0:T(8,128)(2,1)S(1)}, bf16[128,2048]{1,0:T(8,128)(2,1)}, u32[]{:S(2)}) copy-start(bf16[128,2048]{1,0:T(8,128)(2,1)} %get-tuple-element.8) | copy-start | bytes 1572868
  108.6 3.6 %copy-start = (bf16[128,4096]{1,0:T(8,128)(2,1)S(1)}, bf16[128,4096]{1,0:T(8,128)(2,1)}, u32[]{:S(2)}) copy-start(bf16[128,4096]{1,0:T(8,128)(2,1)} %get-tuple-element.10) | copy-start | bytes 3145732
  110.5 1.0 copy-start.2

commit v3 on v2

--- a/solution.py
+++ b/solution.py
@@ -309,6 +309,33 @@
         for copy in vx:
             copy.start()
 
+    for b in range(4):
+        kt[0, :, b * CHUNK : (b + 1) * CHUNK] = kchunk(kbuf, 0, b).T
+
+    def across(buf):
+        rows = [aligned(yfrom[d], 128) for d in range(4)]
+        return [rc(buf.at[1, c, r], buf.at[1, c, r], sib) for r in rows]
+
+    kxs = across(kbuf)
+    vxs = rc(vbuf.at[1, c], vbuf.at[1, c], sib)
+
+    @pl.when(upper)
+    def _():
+        for d in range(4):
+            kx[d].wait_recv()
+            kxs[d].start()
+            kxs[d].wait_recv()
+            part = kchunk(kbuf, 1, yfrom[d])
+            kt[1, :, aligned(yfrom[d], CHUNK)] = part.T
+
+            def body(b, carry):
+                sc = nt(part, qs[b])
+                sbuf[b, aligned(yfrom[d] + 4, CHUNK), :] = sc
+                stat[b] = jnp.maximum(stat[b], fold8(sc, jnp.max))
+                return carry
+
+            lax.fori_loop(0, 4, body, 0)
+
     for d in range(4):
         uc[d].wait_recv()
     nc = [
@@ -326,34 +353,6 @@
         for hd in range(4):
             cols = slice(hd * 128, hd * 128 + 128)
             ust[b, :, cols] = ubuf[b, :, cols].T
-        kt[0, :, b * CHUNK : (b + 1) * CHUNK] = kchunk(kbuf, 0, b).T
-    vsib.wait_recv()
-    for b in range(4):
-        vt[0, :, b * CHUNK : (b + 1) * CHUNK] = kchunk(vbuf, 0, b).T
-
-    def across(buf):
-        rows = [aligned(yfrom[d], 128) for d in range(4)]
-        return [rc(buf.at[1, c, r], buf.at[1, c, r], sib) for r in rows]
-
-    kxs = across(kbuf)
-    vxs = rc(vbuf.at[1, c], vbuf.at[1, c], sib)
-
-    @pl.when(upper)
-    def _():
-        for d in range(4):
-            kx[d].wait_recv()
-            kxs[d].start()
-            kxs[d].wait_recv()
-            part = kchunk(kbuf, 1, yfrom[d])
-            kt[1, :, aligned(yfrom[d], CHUNK)] = part.T
-
-            def body(b, carry):
-                sc = nt(part, qs[b])
-                sbuf[b, aligned(yfrom[d] + 4, CHUNK), :] = sc
-                stat[b] = jnp.maximum(stat[b], fold8(sc, jnp.max))
-                return carry
-
-            lax.fori_loop(0, 4, body, 0)
 
     for b in range(4):
         shift = jnp.max(stat[b], axis=0, keepdims=True) * (FACTOR * LOG2E)
@@ -435,6 +434,10 @@
             vt[1, :, j * CHUNK : (j + 1) * CHUNK] = kchunk(vbuf, 1, j).T
 
     forward_w(upper, 0)
+
+    vsib.wait_recv()
+    for b in range(4):
+        vt[0, :, b * CHUNK : (b + 1) * CHUNK] = kchunk(vbuf, 0, b).T
 
     def by_keys(t, b):
         def far(_, total):
@@ -607,14 +610,6 @@
         out_gn.append(lc(gns.at[r, my_rows], gn_o.at[:, cols]))
         out_gn[r].start()
 
-    @pl.when(lower)
-    def _():
-        dkx.wait_recv()
-        dkfin[...] = (
-            (dkown[0] + dksib[0].astype(F32)) * FACTOR + dkcr[...].astype(F32)
-        ).astype(BF16)
-        send_dk()
-
     my_piece = aligned(i, 32)
     total = tfull[aligned(za, 32), :].astype(F32)
     for copy in z2[0] + z2[1]:
@@ -635,6 +630,14 @@
     out_dw = [lc(zfin.at[p], dw_o.at[p]) for p in (my_piece, far_piece)]
     for copy in out_dw:
         copy.start()
+    @pl.when(lower)
+    def _():
+        dkx.wait_recv()
+        dkfin[...] = (
+            (dkown[0] + dksib[0].astype(F32)) * FACTOR + dkcr[...].astype(F32)
+        ).astype(BF16)
+        send_dk()
+
     for copy in pc + pf:
         copy.wait_recv()
 

time: 114 us -> 115 us (level); the launches traced: 113 us -> 113 us
  no operation moved by 1% of the time
where the time goes in v3:
time: 115 us; the launch traced here: 113 us
  Pallas kernels  108 us (94%)
  local copies, waits for them, and re-layouts  2.66 us (2%)
  other arithmetic  1.92 us (2%)
    pallas_call x1, Pallas kernels, local(): pl.pallas_call(kernel, out_shape=(jax.ShapeDtypeStruct((128, 2048), BF16)...  108 us
    unnamed x9, local copies, waits for them, and re-layouts  2.66 us

profile of v3, /device:TPU:6, one launch (start us, length us, event | category | flops | bytes accessed | tf_op | source)
XLA Modules:
  0.0 112.8 jit_solution(16731306202937674833)
XLA Ops:
  0.6 107.6 %shard_map.93 = (bf16[128,2048]{1,0:T(8,128)(2,1)}, bf16[128,512]{1,0:T(8,128)(2,1)}, bf16[128,4096]{1,0:T(8,128)(2,1)}, bf16[256,512]{1,0:T(8,128)(2,1)}) custom-call(bf16[128,2048]{1,0:T(8,128)(2,1)} %bitcast.16, bf16[128,512]{1,0:T(8,128)(2,1)} %bitcast.19, bf16[128,512]{1,0:T(8,128)(2,1)} %bitcast.20, bf16[128,2048]{1,0:T(8,128)(2,1)} %bitcast.17, ...), custom_call_target="tpu_custom_call" | custom-call | flops 6000000000 | bytes 5000000 | tf_op jit(solution)/shard_map/pallas_call | solution.py:677
  108.2 0.0 copy-start.1
  108.2 0.0 copy-start
  108.3 1.9 %bitcast_convert_fusion = f32[1,256,512]{2,1,0:T(8,128)} fusion(bf16[256,512]{1,0:T(8,128)(2,1)} %get-tuple-element.11), kind=kLoop, calls=%fused_computation | loop fusion | flops 131072 | bytes 786432 | tf_op jit(solution)/shard_map/broadcast_in_dim | solution.py:733
  110.2 0.0 copy-done.1
  110.2 0.0 copy-start.2
  110.2 0.8 copy.13
  111.0 0.2 copy-done.2
  111.2 0.7 copy.14
  111.9 0.0 copy-done
  111.9 1.0 copy.15
Async XLA Ops:
  108.2 1.9 %copy-start.1 = (bf16[128,2048]{1,0:T(8,128)(2,1)S(1)}, bf16[128,2048]{1,0:T(8,128)(2,1)}, u32[]{:S(2)}) copy-start(bf16[128,2048]{1,0:T(8,128)(2,1)} %get-tuple-element.8) | copy-start | bytes 1572868
  108.2 3.6 %copy-start = (bf16[128,4096]{1,0:T(8,128)(2,1)S(1)}, bf16[128,4096]{1,0:T(8,128)(2,1)}, u32[]{:S(2)}) copy-start(bf16[128,4096]{1,0:T(8,128)(2,1)} %get-tuple-element.10) | copy-start | bytes 3145732
  110.2 1.0 copy-start.2

commit v4 on v3

--- a/solution.py
+++ b/solution.py
@@ -193,8 +193,6 @@
     qc = [
         rc(q_ref.at[:, aligned(ys[d], GROUP)], qbuf.at[y], ydev(d)) for d in range(1, 4)
     ]
-    for copy in qc:
-        go(copy)
     vx = crossing(v_ref, vbuf)
     uc = [
         rc(
@@ -204,8 +202,6 @@
         )
         for d in range(4)
     ]
-    for copy in uc:
-        go(copy)
 
     for d in range(1, 4):
         kc[d - 1].wait_recv()
@@ -217,6 +213,8 @@
     own_k.wait()
     ksib = rc(kbuf.at[0, c], kbuf.at[0, c], sib)
     go(ksib)
+    for copy in qc + uc:
+        go(copy)
     for d in range(1, 4):
         qc[d - 1].wait_recv()
     own_q.wait()

time: 115 us -> 116 us (level)
    pallas_call x1, Pallas kernels: 108 us -> 109 us  [local(): pl.pallas_call(kernel, out_shape=(jax.ShapeDtypeStruct((128, 2048), BF16)...]
where the time goes in v4:
time: 116 us; the launch traced here: 114 us
  Pallas kernels  109 us (94%)
  local copies, waits for them, and re-layouts  2.66 us (2%)
  other arithmetic  1.92 us (2%)
    pallas_call x1, Pallas kernels, local(): pl.pallas_call(kernel, out_shape=(jax.ShapeDtypeStruct((128, 2048), BF16)...  109 us
    unnamed x9, local copies, waits for them, and re-layouts  2.66 us

profile of v4, /device:TPU:6, one launch (start us, length us, event | category | flops | bytes accessed | tf_op | source)
XLA Modules:
  0.0 114.4 jit_solution(10695785183853482014)
XLA Ops:
  0.6 109.1 %shard_map.93 = (bf16[128,2048]{1,0:T(8,128)(2,1)}, bf16[128,512]{1,0:T(8,128)(2,1)}, bf16[128,4096]{1,0:T(8,128)(2,1)}, bf16[256,512]{1,0:T(8,128)(2,1)}) custom-call(bf16[128,2048]{1,0:T(8,128)(2,1)} %bitcast.16, bf16[128,512]{1,0:T(8,128)(2,1)} %bitcast.19, bf16[128,512]{1,0:T(8,128)(2,1)} %bitcast.20, bf16[128,2048]{1,0:T(8,128)(2,1)} %bitcast.17, ...), custom_call_target="tpu_custom_call" | custom-call | flops 6000000000 | bytes 5000000 | tf_op jit(solution)/shard_map/pallas_call | solution.py:675
  109.8 0.0 copy-start.1
  109.8 0.0 copy-start
  109.8 1.9 %bitcast_convert_fusion = f32[1,256,512]{2,1,0:T(8,128)} fusion(bf16[256,512]{1,0:T(8,128)(2,1)} %get-tuple-element.11), kind=kLoop, calls=%fused_computation | loop fusion | flops 131072 | bytes 786432 | tf_op jit(solution)/shard_map/broadcast_in_dim | solution.py:731
  111.7 0.0 copy-done.1
  111.7 0.0 copy-start.2
  111.7 0.8 copy.13
  112.5 0.2 copy-done.2
  112.7 0.7 copy.14
  113.4 0.0 copy-done
  113.4 1.0 copy.15
Async XLA Ops:
  109.8 1.9 %copy-start.1 = (bf16[128,2048]{1,0:T(8,128)(2,1)S(1)}, bf16[128,2048]{1,0:T(8,128)(2,1)}, u32[]{:S(2)}) copy-start(bf16[128,2048]{1,0:T(8,128)(2,1)} %get-tuple-element.8) | copy-start | bytes 1572868
  109.8 3.6 %copy-start = (bf16[128,4096]{1,0:T(8,128)(2,1)S(1)}, bf16[128,4096]{1,0:T(8,128)(2,1)}, u32[]{:S(2)}) copy-start(bf16[128,4096]{1,0:T(8,128)(2,1)} %get-tuple-element.10) | copy-start | bytes 3145732
  111.7 1.0 copy-start.2
